TPU v7x, 32 devices: a whole 2x2x4 slice. The times are simulated.
32 devices in a mesh: groups: 2 (over y), tm: 4 (over z), cuts: 2 (over x), col: 2 (over core).
Axes of the slice: x: 2, y: 2, z: 4, core: 2. Of those that a mesh axis runs over, the one named last changes fastest.
Arguments:
- turns: bfloat16 [4096, 4, 1280], P(('groups', 'tm'), 'cuts', 'col'), parts along dimension 0, may hold values from -25 to 25
- shifts: int32 [8], P(('groups', 'tm')), parts along dimension 0, may hold values from -16 to 16
- bands: int32 [8], P(('groups', 'cuts')), parts along dimension 0, may hold values from 2 to 24
- memory: float32 [8], P(('groups', 'cuts')), parts along dimension 0, may hold values from 0.8 to 0.995
Outputs:
- filtered: bfloat16 [8192, 4, 1280], P(('groups', 'tm', 'col'), 'cuts'), parts along dimension 0
There are 2 independent parts, one for each index of `groups`. A program takes and returns all parts, laid end to end along the dimension named above; each array names one. Nothing has to cross between parts.
All inputs are finite; a program needn't handle non-finite values.
Results may differ from a plain program's by a relative error of at most 0.015.
The roundings to bfloat16 on the way count: a program that leaves them out, or rounds other values in their place, can miss the bound.
Values may be sent and summed in bfloat16 or wider, within the bound.
A program may use at most 64 MiB of HBM per device.

v0:
```python
import math

import jax
import jax.numpy as jnp
from jax import lax
from jax.sharding import PartitionSpec as P

COLUMNS = 1280
BAND_FREQS = 64


def from_behind(block, axis, distance):
    devices = range(lax.axis_size(axis))
    route = [(i - distance, i) for i in devices if i - distance in devices]
    return lax.ppermute(block, axis, route)


def extended(shard, sides, width):
    for axis, dim in sides:
        devices, length = (lax.axis_size(axis), shard.shape[dim])
        up = [(i, (i + 1) % devices) for i in range(devices - 1)]
        down = [(j, i) for i, j in up]
        last = lax.slice_in_dim(shard, length - width, length, axis=dim)
        leading = lax.slice_in_dim(shard, 0, width, axis=dim)
        before = lax.ppermute(last, axis, up)
        after = lax.ppermute(leading, axis, down)
        shard = jnp.concatenate([before, shard, after], axis=dim)
    return shard


def wave_table(angle_count, freq_count):
    freq_index = lax.broadcasted_iota(jnp.int32, (freq_count, angle_count), 0) + 1
    angle_index = lax.broadcasted_iota(jnp.int32, (freq_count, angle_count), 1)
    phase_int = freq_index * angle_index % angle_count
    radians = phase_int.astype(jnp.float32) * (2.0 * math.pi / angle_count)
    return jnp.concatenate([jnp.cos(radians), jnp.sin(radians)], axis=0).astype(jnp.bfloat16)


def damping_weights(bands, freq_count, angle_count):
    freq_values = (jnp.arange(freq_count, dtype=jnp.int32) + 1).astype(jnp.float32)
    band_width = bands.astype(jnp.float32)
    gaussian = jnp.exp(-freq_values[:, None] ** 2 / (2.0 * band_width[None, :] ** 2)) * (
        2.0 / angle_count
    )
    return jnp.concatenate([gaussian, gaussian], axis=0)


def ramp_table(width_total, offset):
    source_col = lax.broadcasted_iota(jnp.int32, (width_total, width_total), 0)
    target_col = lax.broadcasted_iota(jnp.int32, (width_total, width_total), 1)
    lag_index = (target_col - source_col - offset) % width_total
    distance = jnp.minimum(lag_index, width_total - lag_index)
    dist_float = jnp.maximum(distance, 1).astype(jnp.float32)
    tap_value = jnp.where(
        distance == 0, 0.25, jnp.where(distance % 2 == 1, -1.0 / (math.pi**2 * dist_float**2), 0.0)
    )
    return tap_value.astype(jnp.bfloat16)


def local(turns, shifts, bands, memory):
    half_len, row_count, col_width = turns.shape
    angle_count = 2 * half_len
    spread = row_count * col_width
    wave_rows = wave_table(angle_count, BAND_FREQS)
    older_half = from_behind(turns, "tm", 1)
    flat_own = turns.reshape(half_len, spread)
    flat_old = older_half.reshape(half_len, spread)
    window = jnp.concatenate([flat_old, flat_own], axis=0)
    spectrum = jnp.dot(wave_rows, window, preferred_element_type=jnp.float32)
    column_sum = jnp.sum(window, axis=0, dtype=jnp.float32)
    profile = (column_sum / angle_count).reshape(row_count, col_width)
    decay_rate = memory.reshape(row_count, 1)
    tm_count = lax.axis_size("tm")
    tm_index = lax.axis_index("tm")
    lag_steps = tm_index - jnp.arange(tm_count, dtype=jnp.int32)
    lag_float = jnp.maximum(lag_steps, 0).astype(jnp.float32)
    powers = jnp.where(
        lag_steps[:, None] >= 0, jnp.power(decay_rate[:, 0][None, :], lag_float[:, None]), 0.0
    )
    weight = jnp.sum(powers, axis=0)[:, None]
    all_profiles = lax.all_gather(profile, "tm", axis=0, tiled=True)
    stacked = all_profiles.reshape(tm_count, row_count, col_width)
    weighted_sum = jnp.einsum("ur,urc->rc", powers, stacked, precision=lax.Precision.HIGHEST)
    estimate = weighted_sum / weight
    padded = extended(estimate, (("cuts", 0),), 1)
    smooth = (padded[:-2] + 2.0 * padded[1:-1] + padded[2:]) * 0.25
    weights = damping_weights(bands, BAND_FREQS, angle_count)
    scaled = (spectrum.reshape(2 * BAND_FREQS, row_count, col_width) * weights[:, :, None]).astype(
        jnp.bfloat16
    )
    low = jnp.dot(
        wave_rows.T, scaled.reshape(2 * BAND_FREQS, spread), preferred_element_type=jnp.float32
    )
    damped = (window - low - smooth.reshape(1, spread)).astype(jnp.bfloat16)
    damped = damped.reshape(angle_count, row_count, col_width)
    kernel = ramp_table(COLUMNS, shifts[0])
    row_block = lax.all_to_all(damped, "col", split_axis=0, concat_axis=2, tiled=True)
    lead_rows, item_count, full_width = row_block.shape
    result = jnp.dot(
        row_block.reshape(lead_rows * item_count, full_width),
        kernel,
        preferred_element_type=jnp.float32,
    )
    return result.reshape(lead_rows, item_count, full_width).astype(jnp.bfloat16)


def solution(mesh):
    placed = (
        P(("groups", "tm"), "cuts", "col"),
        P(("groups", "tm")),
        P(("groups", "cuts")),
        P(("groups", "cuts")),
    )
    return jax.shard_map(
        local,
        mesh=mesh,
        in_specs=placed,
        out_specs=P(("groups", "tm", "col"), "cuts", None),
        check_vma=False,
    )
```

profile of v0, /device:TPU:0, one launch (start us, length us, event | category | flops | bytes accessed | tf_op | source)
XLA Modules:
  0.0 95.8 jit_solution(11461236508998719598)
XLA Ops:
  0.0 0.0 copy-start.2
  0.0 5.1 %collective-permute-start = (bf16[512,2,640]{2,1,0:T(2,128)(2,1)}, bf16[512,2,640]{2,1,0:T(2,128)(2,1)S(1)}, u32[]{:S(2)}, u32[]{:S(2)}) collective-permute-start(bf16[512,2,640]{2,1,0:T(2,128)(2,1)} %param.4), channel_id=1, source_target_pairs={{0,4},{4,8},{8,12},{1,5},{5,9},{9,13},{2,6},{6,10},{10,14},{3,7},{... | collective-permute-start | bytes 3932168 | tf_op jit(solution)/shard_map/ppermute | solution.py:15
  5.1 2.6 %copy.17 = bf16[64,8,2,640]{3,1,2,0:T(8,128)(2,1)} copy(bf16[64,8,2,640]{3,2,1,0:T(2,128)(2,1)} %bitcast.30) | data formatting | bytes 2621440
  7.8 0.0 copy-done.2
  7.8 0.1 fusion.37
  7.9 0.0 copy-done.1
  7.9 0.2 fusion.49
  8.1 1.2 %cosine_convert_fusion = (bf16[64,1024]{1,0:T(8,128)(2,1)S(1)}, bf16[64,1024]{1,0:T(8,128)(2,1)S(1)}) fusion(s32[64]{0:T(128)S(1)} %iota_add_fusion), kind=kLoop, calls=%fused_computation.41 | loop fusion | flops 1048576 | bytes 262400 | tf_op jit(solution)/shard_map/convert
  9.3 24.1 %collective-permute-done = bf16[512,2,640]{2,1,0:T(2,128)(2,1)S(1)} collective-permute-done((bf16[512,2,640]{2,1,0:T(2,128)(2,1)}, bf16[512,2,640]{2,1,0:T(2,128)(2,1)S(1)}, u32[]{:S(2)}, u32[]{:S(2)}) %collective-permute-start) | collective-permute-done | bytes 1310752 | tf_op jit(solution)/shard_map/ppermute | solution.py:15
  33.4 0.2 copy.16
  33.6 0.1 constant_dynamic-update-slice_fusion.1
  33.7 1.0 %copy-done = bf16[64,8,2,640]{3,1,2,0:T(8,128)(2,1)S(1)} copy-done((bf16[64,8,2,640]{3,1,2,0:T(8,128)(2,1)S(1)}, bf16[64,8,2,640]{3,1,2,0:T(8,128)(2,1)}, u32[]{:S(2)}) %copy-start) | copy-done | bytes 1310744
  34.7 0.1 constant_dynamic-update-slice_fusion
  34.8 0.4 convert_reduce_fusion
  35.2 14.2 %all-gather = f32[4,2,640]{2,1,0:T(2,128)S(1)} all-gather(f32[1,2,640]{2,1,0:T(2,128)S(1)} %reshape.55), channel_id=1, replica_groups=mesh['groups'=2,'tm'=4,'cuts'=2,'col'=2] {'tm'}, dimensions={0}, use_global_device_ids=true | all-gather | bytes 25600 | tf_op jit(solution)/shard_map/all_gather | solution.py:81
  49.4 0.2 fusion.32
  49.6 0.1 bitcast_divide_fusion
  49.7 1.3 %collective-permute-start.2 = (f32[1,640]{1,0:T(1,128)S(1)}, f32[1,640]{1,0:T(1,128)}, u32[]{:S(2)}, u32[]{:S(2)}) collective-permute-start(f32[1,640]{1,0:T(1,128)S(1)} %get-tuple-element.8), channel_id=1, source_target_pairs={{2,0},{3,1},{6,4},{7,5},{10,8},{11,9},{14,12},{15,13},{18,16},{19,... | collective-permute-start | bytes 7688 | tf_op jit(solution)/shard_map/ppermute | solution.py:26
  51.0 5.7 %collective-permute-start.1 = (f32[1,640]{1,0:T(1,128)S(1)}, f32[1,640]{1,0:T(1,128)}, u32[]{:S(2)}, u32[]{:S(2)}) collective-permute-start(f32[1,640]{1,0:T(1,128)S(1)} %get-tuple-element.7), channel_id=1, source_target_pairs={{0,2},{1,3},{4,6},{5,7},{8,10},{9,11},{12,14},{13,15},{16,18},{17,... | collective-permute-start | bytes 7688 | tf_op jit(solution)/shard_map/ppermute | solution.py:25
  56.6 0.1 pad_maximum_fusion.2
  56.7 0.1 copy.10
  56.8 0.2 mul.58
  57.8 0.0 collective-permute-done.2
  57.8 0.0 collective-permute-done.1
  57.8 0.7 fusion.35
  58.5 2.7 %fusion.7 = bf16[1024,1280]{1,0:T(8,128)(2,1)} fusion(bf16[1024,1280]{1,0:T(8,128)(2,1)S(1)} %constant_dynamic-update-slice_fusion, f32[1280]{0:T(1024)S(1)} %sub.42, f32[128,1280]{1,0:T(8,128)S(1)} %bitcast.32, bf16[64,1024]{1,0:T(8,128)(2,1)S(1)} %get-tuple-element.10, bf16[64,1024]{1,0:T(8,128)(2,1)S(1)} %get-tuple-element.9), kind=kOutput, calls=%fused_computation.16 | convolution fusion | flops 677707776 | bytes 6165504 | tf_op jit(solution)/shard_map/dot_general | solution.py:91
  61.2 5.1 %reshape.54 = bf16[1024,2,640]{2,1,0:T(2,128)(2,1)S(1)} reshape(bf16[1024,1280]{1,0:T(8,128)(2,1)} %fusion.7) | data formatting | bytes 5242880 | tf_op jit(solution)/shard_map/reshape | solution.py:95
  66.3 5.8 %all_to_all.15 = bf16[1024,2,640]{2,1,0:T(2,128)(2,1)S(1)} all-to-all(bf16[1024,2,640]{2,1,0:T(2,128)(2,1)S(1)} %reshape.54), channel_id=1, replica_groups=mesh['groups'=2,'tm'=4,'cuts'=2,'col'=2] {'col'}, dimensions={0} | all-to-all | bytes 5242880 | tf_op jit(solution)/shard_map/all_to_all | solution.py:97
  72.1 2.7 %copy.23 = bf16[2,512,2,640]{3,0,1,2:T(2,128)(2,1)S(1)} copy(bf16[2,512,2,640]{3,2,1,0:T(2,128)(2,1)S(1)} %bitcast.25) | data formatting | bytes 5242880 | tf_op jit(solution)/shard_map/all_to_all | solution.py:97
  74.8 2.9 %dot_general.17 = bf16[512,2,1280]{2,0,1:T(8,128)(2,1)} reshape(bf16[512,2,2,640]{3,2,0,1:T(2,128)(2,1)S(1)} %bitcast.26) | data formatting | bytes 5242880 | tf_op jit(solution)/shard_map/dot_general | solution.py:99
  77.8 13.8 %convolution_convert_fusion = bf16[512,2,1280]{2,0,1:T(8,128)(2,1)S(1)} fusion(bf16[512,2,1280]{2,0,1:T(8,128)(2,1)} %dot_general.17, s32[]{:T(128)} %bitcast.24), kind=kOutput, calls=%fused_computation.17 | convolution fusion | flops 3407544320 | bytes 5242884 | tf_op jit(solution)/shard_map/dot_general | solution.py:99
  91.6 4.2 %copy.12 = bf16[512,2,1280]{2,1,0:T(2,128)(2,1)} copy(bf16[512,2,1280]{2,0,1:T(8,128)(2,1)S(1)} %convolution_convert_fusion) | data formatting | bytes 5242880 | tf_op jit(solution)/shard_map/convert_element_type | solution.py:104
  (12 shorter events, 0.1 us)
Async XLA Ops:
  0.0 7.8 %copy-start.2 = (s32[2]{0:T(128)S(1)}, s32[2]{0:T(128)}, u32[]{:S(2)}) copy-start(s32[2]{0:T(128)} %param.6) | copy-start | bytes 28
  0.0 7.9 %copy-start.1 = (f32[2]{0:T(128)S(1)}, f32[2]{0:T(128)}, u32[]{:S(2)}) copy-start(f32[2]{0:T(128)} %param.7) | copy-start | bytes 28
  0.0 33.4 %collective-permute-start = (bf16[512,2,640]{2,1,0:T(2,128)(2,1)}, bf16[512,2,640]{2,1,0:T(2,128)(2,1)S(1)}, u32[]{:S(2)}, u32[]{:S(2)}) collective-permute-start(bf16[512,2,640]{2,1,0:T(2,128)(2,1)} %param.4), channel_id=1, source_target_pairs={{0,4},{4,8},{8,12},{1,5},{5,9},{9,13},{2,6},{6,10},{10,14},{3,7},{... | collective-permute-start | bytes 3932168 | tf_op jit(solution)/shard_map/ppermute | solution.py:15
  33.4 1.3 %copy-start = (bf16[64,8,2,640]{3,1,2,0:T(8,128)(2,1)S(1)}, bf16[64,8,2,640]{3,1,2,0:T(8,128)(2,1)}, u32[]{:S(2)}) copy-start(bf16[64,8,2,640]{3,1,2,0:T(8,128)(2,1)} %copy.17) | copy-start | bytes 3932164
  49.7 8.1 %collective-permute-start.2 = (f32[1,640]{1,0:T(1,128)S(1)}, f32[1,640]{1,0:T(1,128)}, u32[]{:S(2)}, u32[]{:S(2)}) collective-permute-start(f32[1,640]{1,0:T(1,128)S(1)} %get-tuple-element.8), channel_id=1, source_target_pairs={{2,0},{3,1},{6,4},{7,5},{10,8},{11,9},{14,12},{15,13},{18,16},{19,... | collective-permute-start | bytes 7688 | tf_op jit(solution)/shard_map/ppermute | solution.py:26
  51.0 6.8 %collective-permute-start.1 = (f32[1,640]{1,0:T(1,128)S(1)}, f32[1,640]{1,0:T(1,128)}, u32[]{:S(2)}, u32[]{:S(2)}) collective-permute-start(f32[1,640]{1,0:T(1,128)S(1)} %get-tuple-element.7), channel_id=1, source_target_pairs={{0,2},{1,3},{4,6},{5,7},{8,10},{9,11},{12,14},{13,15},{16,18},{17,... | collective-permute-start | bytes 7688 | tf_op jit(solution)/shard_map/ppermute | solution.py:25
where the time goes:
time: 96.2 us; the launch traced here: 95.8 us
  waiting for transfers between devices  24.1 us (25%)
  blocking collectives  20 us (21%)
  local copies, waits for them, and re-layouts  19.3 us (20%)
  matrix products  16.7 us (17%)
  starting transfers between devices  12.1 us (13%)
  other arithmetic  2.81 us (3%)
    ppermute x1, waiting for transfers between devices, from_behind(): return lax.ppermute(block, axis, route)  24.1 us
    all_gather x1, blocking collectives, local(): all_profiles = lax.all_gather(profile, 'tm', axis=0, tiled=True)  14.2 us
    dot_general x1, matrix products, local(): jnp.dot(row_block.reshape(lead_rows * item_count, full_width), kernel, pr...  13.8 us
    all_to_all x1, blocking collectives, local(): lax.all_to_all(damped, 'col', split_axis=0, concat_axis=2, tiled=True)  5.84 us
    ppermute x1, starting transfers between devices, extended(): before = lax.ppermute(last, axis, up)  5.68 us
    ppermute x1, starting transfers between devices, from_behind(): return lax.ppermute(block, axis, route)  5.13 us
    reshape x1, local copies, waits for them, and re-layouts, local(): damped = damped.reshape(angle_count, row_count, col_width)  5.07 us
    convert_element_type x1, local copies, waits for them, and re-layouts, local(): result.reshape(lead_rows, item_count, full_width).astype(jnp.bfloat16)  4.19 us
  transfers between devices with their start and end apart: 3, of which 1 were waited for; matrix products, arithmetic and copies ran while one was open for 5% of the time, Pallas kernels for 0%

commit v1 on v0

v1 whole, which is shorter than its diff:
```python
import functools
import math

import jax
import jax.numpy as jnp
import ml_dtypes
import numpy as np
from jax import lax
from jax.experimental import pallas as pl
from jax.experimental.pallas import tpu as pltpu
from jax.sharding import PartitionSpec as P

BAND_FREQS = 64
MESH = pl.DeviceIdType.MESH
LANES = 128
F32 = jnp.float32
BF16 = jnp.bfloat16


def tables(half_len, row_count):
    angle_count = 2 * half_len
    freq = np.arange(1, BAND_FREQS + 1, dtype=np.int64)[:, None]
    phase = (freq * np.arange(half_len, dtype=np.int64)[None, :]) % angle_count
    radians = phase.astype(np.float64) * (2.0 * math.pi / angle_count)
    waves = np.concatenate([np.cos(radians), np.sin(radians)], axis=0)
    count = 2 * BAND_FREQS
    wide = np.zeros((row_count, count, half_len, row_count), np.float64)
    ones = np.zeros((16, half_len, row_count), np.float64)
    for s in range(row_count):
        wide[s, :, :, s] = waves
        ones[s, :, s] = 1.0
    wide = wide.reshape(row_count * count, half_len * row_count)
    ones = ones.reshape(16, half_len * row_count)
    cast = lambda v: jnp.asarray(v.astype(np.float32).astype(ml_dtypes.bfloat16))
    return cast(wide), cast(wide.T), cast(ones)


def kernel(sizes, x_ref, wave_ref, wave_t_ref, ones_ref, gain_ref, coef_ref, base_ref, out_ref,
           held, part, other, ramp, acc, sums, est, near, cyc,
           z_send, c_send, recv, p_send, p_recv, s_send, s_recv, e_send, e_recv):
    T, C, R = sizes
    rows, width = x_ref.shape
    chunks = width // LANES
    total = 2 * width
    tm = lax.axis_index("tm")
    cut = lax.axis_index("cuts")
    col = lax.axis_index("col")
    mate = 1 - col

    sums[tm] = jnp.dot(ones_ref[...], x_ref[...], preferred_element_type=F32)[:8]

    barrier = pltpu.get_barrier_semaphore()

    def greet(**where):
        pl.semaphore_signal(barrier, inc=1, device_id=where, device_id_type=MESH)

    for step in range(1, T):
        greet(tm=lax.rem(tm + step, T))
    greet(col=mate)
    for delta in (-1, 1):
        @pl.when((cut + delta >= 0) & (cut + delta < C))
        def _():
            for c in range(2):
                greet(cuts=cut + delta, col=jnp.int32(c))
    cross_up = (col == 1) & (tm < T - 1)
    cross_down = (col == 0) & (tm > 0)

    @pl.when(cross_up)
    def _():
        greet(tm=tm + 1, col=jnp.int32(0))

    @pl.when(cross_down)
    def _():
        greet(tm=tm - 1, col=jnp.int32(1))

    one = lambda flag: jnp.where(flag, 1, 0).astype(jnp.int32)
    pl.semaphore_wait(
        barrier, T + 2 * one(cut > 0) + 2 * one(cut < C - 1) + one(cross_up) + one(cross_down)
    )

    def sum_copy(source, target):
        return pltpu.make_async_remote_copy(
            src_ref=sums.at[source], dst_ref=sums.at[source],
            send_sem=s_send.at[target], recv_sem=s_recv.at[source],
            device_id={"tm": target}, device_id_type=MESH)

    for u in range(T):
        @pl.when(u > tm)
        def _():
            sum_copy(tm, jnp.int32(u)).start()

    def bulk(j, source_col, send_sem, where):
        return pltpu.make_async_remote_copy(
            src_ref=x_ref.at[:, pl.ds(pl.multiple_of(j * LANES, LANES), LANES)],
            dst_ref=held.at[j, :, pl.ds(pl.multiple_of(source_col * LANES, LANES), LANES)],
            send_sem=send_sem.at[j], recv_sem=recv.at[source_col, j],
            device_id=where, device_id_type=MESH)

    def ahead(j):
        return bulk(j, col, z_send, {"tm": lax.rem(tm + 1, T), "col": jnp.int32(0)})

    def across(j):
        return bulk(j, jnp.int32(0), c_send, {"col": mate})

    @pl.when(tm < T - 1)
    def _():
        @pl.loop(0, chunks)
        def _(j):
            ahead(j).start()

    @pl.when(col == 0)
    def _():
        @pl.loop(0, chunks)
        def _(j):
            across(j).start()

    @pl.when(col == 1)
    def _():
        for j in range(chunks):
            held[j, :, LANES:] = x_ref[:, j * LANES:(j + 1) * LANES]

    @pl.when((col == 0) & (tm == 0))
    def _():
        held[...] = jnp.zeros_like(held)

    acc[...] = jnp.zeros_like(acc)

    STEP = 32

    @pl.loop(0, chunks)
    def _(j):
        for c in range(2):
            @pl.loop(0, LANES // STEP)
            def _(k):
                m = lax.broadcasted_iota(jnp.int32, (STEP, total), 0) + (
                    c * width + j * LANES + k * STEP)
                lag = base_ref[...] - m
                lag = jnp.where(lag < 0, lag + total, lag)
                dist = jnp.minimum(lag, total - lag)
                wide = jnp.maximum(dist, 1).astype(F32)
                tap = jnp.where(
                    dist == 0, 0.25,
                    jnp.where((dist & 1) == 1, -1.0 / (math.pi**2 * wide * wide), 0.0))
                ramp[j, pl.ds(pl.multiple_of(c * LANES + k * STEP, STEP), STEP), :] = tap.astype(BF16)

    est[...] = jnp.zeros_like(est)
    for u in range(T):
        @pl.when(u < tm)
        def _():
            sum_copy(jnp.int32(u), lax.rem(tm + 1, T)).wait_recv()

        @pl.when(u <= tm)
        def _():
            est[...] += coef_ref[u] * sums[u]
    near[1, col] = est[...]

    def est_copy(delta, to_col, from_col):
        return pltpu.make_async_remote_copy(
            src_ref=est, dst_ref=near.at[1 - delta, from_col],
            send_sem=e_send.at[1 - delta, to_col], recv_sem=e_recv.at[1 - delta, from_col],
            device_id={"cuts": cut + delta, "col": to_col}, device_id_type=MESH)

    est_copy(0, mate, col).start()
    for delta in (-1, 1):
        @pl.when((cut + delta >= 0) & (cut + delta < C))
        def _():
            for c in range(2):
                est_copy(delta, jnp.int32(c), col).start()

    def part_copy(j):
        return pltpu.make_async_remote_copy(
            src_ref=part.at[j], dst_ref=other.at[j],
            send_sem=p_send.at[j], recv_sem=p_recv.at[j],
            device_id={"col": mate}, device_id_type=MESH)

    def gather(j):
        @pl.when((col == 1) | (tm > 0))
        def _():
            bulk(j, jnp.int32(0), z_send, {"col": mate}).wait_recv()

        @pl.when((col == 0) & (tm > 0))
        def _():
            bulk(j, jnp.int32(1), z_send, {"col": mate}).wait_recv()

        part[j] = jnp.dot(wave_ref[...], held[j], preferred_element_type=F32)
        part_copy(j).start()

    gather(0)

    est_copy(0, mate, mate).wait_recv()
    for delta in (-1, 1):
        @pl.when((cut - delta >= 0) & (cut - delta < C))
        def _():
            for c in range(2):
                pltpu.make_async_remote_copy(
                    src_ref=est, dst_ref=near.at[1 - delta, c],
                    send_sem=e_send.at[1 - delta, c], recv_sem=e_recv.at[1 - delta, c],
                    device_id={"cuts": cut - delta, "col": jnp.int32(c)},
                    device_id_type=MESH).wait_recv()

        @pl.when((cut - delta < 0) | (cut - delta >= C))
        def _():
            near[1 - delta] = jnp.zeros_like(near[1 - delta])

    for c in range(2):
        edge = [near[0, c, R - 1:R, :]] + [near[1, c, s:s + 1, :] for s in range(R)] + [near[2, c, 0:1, :]]
        for s in range(R):
            line = (edge[s] + 2.0 * edge[s + 1] + edge[s + 2]) * 0.25
            for j in range(chunks):
                cyc[j, s:s + 1, c * LANES:(c + 1) * LANES] = line[:, j * LANES:(j + 1) * LANES]

    TILE = 256

    def filt(j, last):
        part_copy(j).wait_recv()
        scaled = (gain_ref[0] * part[j] + gain_ref[1] * other[j]).astype(BF16)
        which = lax.broadcasted_iota(jnp.int32, (TILE, 2 * LANES), 0) % R
        shade = jnp.zeros((TILE, 2 * LANES), F32)
        for s in range(R):
            shade = jnp.where(which == s, cyc[j, s:s + 1, :], shade)

        @pl.loop(0, rows // TILE)
        def _(k):
            tile = pl.ds(pl.multiple_of(k * TILE, TILE), TILE)
            low = jnp.dot(wave_t_ref[tile, :], scaled, preferred_element_type=F32)
            damped = (held[j, tile, :].astype(F32) - low - shade).astype(BF16)
            product = acc[tile, :] + jnp.dot(damped, ramp[j], preferred_element_type=F32)
            if last:
                out_ref[tile, :] = product.astype(BF16)
            else:
                acc[tile, :] = product

    @pl.loop(1, chunks)
    def _(j):
        gather(j)
        filt(j - 1, False)

    filt(chunks - 1, True)

    for u in range(T):
        @pl.when(u > tm)
        def _():
            sum_copy(tm, jnp.int32(u)).wait_send()
    est_copy(0, mate, col).wait_send()
    for delta in (-1, 1):
        @pl.when((cut + delta >= 0) & (cut + delta < C))
        def _():
            for c in range(2):
                est_copy(delta, jnp.int32(c), col).wait_send()

    @pl.loop(0, chunks)
    def _(j):
        part_copy(j).wait_send()

        @pl.when(tm < T - 1)
        def _():
            ahead(j).wait_send()

        @pl.when(col == 0)
        def _():
            across(j).wait_send()


def local(turns, shifts, bands, memory):
    half_len, R, width = turns.shape
    T, C = lax.axis_size("tm"), lax.axis_size("cuts")
    tm = lax.axis_index("tm")
    rows, total, chunks = half_len * R, 2 * width, width // LANES
    angle_count = 2 * half_len
    count = 2 * BAND_FREQS
    wide, wide_t, ones = tables(half_len, R)
    flat = turns.reshape(rows, width)

    freq = np.arange(1, BAND_FREQS + 1, dtype=np.float32)
    freq = np.concatenate([freq, freq])
    sign = np.where(freq % 2 == 1, -1.0, 1.0).astype(np.float32)
    gain = jnp.exp(-(freq[None, :] ** 2) / (2.0 * bands.astype(F32)[:, None] ** 2)) * (2.0 / angle_count)
    gains = jnp.stack([gain.reshape(R * count, 1), (gain * sign[None, :]).reshape(R * count, 1)])

    lag = tm - jnp.arange(T + 1, dtype=jnp.int32)
    powers = jnp.where(
        lag[:, None] >= 0,
        jnp.power(memory[None, :], jnp.maximum(lag, 0).astype(F32)[:, None]), 0.0)
    coef = (powers[:-1] + powers[1:]) / (jnp.sum(powers, axis=0)[None, :] * angle_count)
    coef = jnp.pad(coef, ((0, 0), (0, 8 - R)))[:, :, None]
    base = ((jnp.arange(total, dtype=jnp.int32) - shifts[0]) % total)[None, :]

    vmem = pl.BlockSpec(memory_space=pltpu.VMEM)
    dma = pltpu.SemaphoreType.DMA
    out = pl.pallas_call(
        functools.partial(kernel, (T, C, R)),
        out_shape=jax.ShapeDtypeStruct((rows, total), BF16),
        in_specs=[vmem] * 7,
        out_specs=vmem,
        scratch_shapes=[
            pltpu.VMEM((chunks, rows, 2 * LANES), BF16),
            pltpu.VMEM((chunks, R * count, 2 * LANES), F32),
            pltpu.VMEM((chunks, R * count, 2 * LANES), F32),
            pltpu.VMEM((chunks, 2 * LANES, total), BF16),
            pltpu.VMEM((rows, total), F32),
            pltpu.VMEM((T, 8, width), F32),
            pltpu.VMEM((8, width), F32),
            pltpu.VMEM((3, 2, 8, width), F32),
            pltpu.VMEM((chunks, 8, 2 * LANES), F32),
            dma((chunks,)), dma((chunks,)), dma((2, chunks)),
            dma((chunks,)), dma((chunks,)),
            dma((T,)), dma((T,)), dma((3, 2)), dma((3, 2)),
        ],
        compiler_params=pltpu.CompilerParams(
            collective_id=0, has_side_effects=True, vmem_limit_bytes=48 * 1024 * 1024),
        cost_estimate=pl.CostEstimate(
            flops=2 * rows * total * (total + 2 * R * count),
            bytes_accessed=8 * rows * total, transcendentals=0),
    )(flat, wide, wide_t, ones, gains, coef, base)
    return out.reshape(half_len, R, total)


def solution(mesh):
    placed = (
        P(("groups", "tm"), "cuts", "col"),
        P(("groups", "tm")),
        P(("groups", "cuts")),
        P(("groups", "cuts")),
    )
    return jax.shard_map(
        local,
        mesh=mesh,
        in_specs=placed,
        out_specs=P(("groups", "tm", "col"), "cuts", None),
        check_vma=False,
    )
```

time: 96.2 us -> 51.9 us (0.54)
  the two profiles are of different devices: /device:TPU:0 before, /device:TPU:12 now
where the time goes in v1:
time: 51.9 us; the launch traced here: 51.6 us
  Pallas kernels  39.3 us (76%)
  local copies, waits for them, and re-layouts  9.25 us (18%)
  other arithmetic  2.25 us (4%)
  between operations  0.78 us (2%)
    pallas_call x1, Pallas kernels, local(): pl.pallas_call(functools.partial(kernel, (T, C, R)), out_shape=jax.ShapeD...  39.3 us
    reshape x1, local copies, waits for them, and re-layouts, local(): flat = turns.reshape(rows, width)  4.07 us
    reshape x1, local copies, waits for them, and re-layouts, local(): return out.reshape(half_len, R, total)  2.44 us
    unnamed x8, local copies, waits for them, and re-layouts  2.36 us

profile of v1, /device:TPU:12, one launch (start us, length us, event | category | flops | bytes accessed | tf_op | source)
XLA Modules:
  0.0 51.6 jit_solution(4951226136900840561)
XLA Ops:
  0.0 0.0 copy-start.3
  0.0 0.0 copy-start.1
  0.7 0.7 %multiply_multiply_fusion = f32[2]{0:T(128)S(1)} fusion(s32[2]{0:T(128)} %param.11), kind=kLoop, calls=%fused_computation.11 | loop fusion | flops 6 | bytes 16 | tf_op jit(solution)/shard_map/mul | solution.py:277
  1.4 0.8 %broadcast_multiply_fusion.1 = (f32[2,128]{1,0:T(2,128)S(1)}, f32[2,128]{1,0:T(2,128)S(1)}) fusion(f32[2]{0:T(128)S(1)} %multiply_multiply_fusion, f32[128]{0:T(128)} %constant.49, f32[128]{0:T(128)} %constant.51), kind=kLoop, calls=%fused_computation.10 | loop fusion | flops 768 | bytes 3080 | tf_op jit(solution)/shard_map/mul | solution.py:277
  2.1 0.8 %fusion.1 = (f32[2]{0:T(128)S(1)}, f32[5,2]{1,0:T(8,128)S(1)}) fusion(f32[5]{0:T(128)S(1)} %maximum_convert_fusion, f32[2]{0:T(128)} %param.12, pred[5]{0:T(512)(128)(4,1)S(1)} %fusion), kind=kLoop, calls=%fused_computation.12 | loop fusion | flops 18 | bytes 81 | tf_op jit(solution)/shard_map/reduce_sum | solution.py:284
  3.0 0.1 copy.20.coef_ref
  3.1 0.1 copy.19
  3.2 0.1 copy.18
  3.4 4.1 %reshape.107.x_ref = bf16[1024,640]{1,0:T(8,128)(2,1)} reshape(bf16[512,2,640]{2,1,0:T(2,128)(2,1)} %param.9) | data formatting | bytes 2621440 | tf_op jit(solution)/shard_map/reshape | solution.py:272
  7.5 0.0 copy-done.3
  7.5 0.0 copy-done.1
  7.5 0.0 copy-start
  7.5 1.3 %copy-done = bf16[1024,640]{1,0:T(8,128)(2,1)S(1)} copy-done((bf16[1024,640]{1,0:T(8,128)(2,1)S(1)}, bf16[1024,640]{1,0:T(8,128)(2,1)}, u32[]{:S(2)}) %copy-start) | copy-done | bytes 1310744
  8.8 0.0 copy-start.2
  8.8 1.0 %copy-done.2 = bf16[256,1024]{1,0:T(8,128)(2,1)S(1)} copy-done((bf16[256,1024]{1,0:T(8,128)(2,1)S(1)}, bf16[256,1024]{1,0:T(8,128)(2,1)}, u32[]{:S(2)}) %copy-start.2) | copy-done | bytes 524312
  9.8 39.3 %shard_map.91 = bf16[1024,1280]{1,0:T(8,128)(2,1)S(1)} custom-call(bf16[1024,640]{1,0:T(8,128)(2,1)S(1)} %copy-done, bf16[256,1024]{1,0:T(8,128)(2,1)S(1)} %copy-done.2, bf16[1024,256]{1,0:T(8,128)(2,1)S(1)} %copy-done.1, bf16[16,1024]{1,0:T(8,128)(2,1)S(1)} %copy-done.3, f32[2,256,1]{2,1,0:T(8,128)S(1)} %pad_maximum_fusion.gain_ref, ...), custom_call_target="tpu_custom_call" | custom-call | flops 4697620480 | bytes 10485760 | tf_op jit(solution)/shard_map/pallas_call | solution.py:290
  49.1 2.4 %reshape.108 = bf16[512,2,1280]{2,1,0:T(2,128)(2,1)} reshape(bf16[1024,1280]{1,0:T(8,128)(2,1)S(1)} %shard_map.91) | data formatting | bytes 5242880 | tf_op jit(solution)/shard_map/reshape | solution.py:315
  (7 shorter events, 0.1 us)
Async XLA Ops:
  0.0 7.5 %copy-start.3 = (bf16[16,1024]{1,0:T(8,128)(2,1)S(1)}, bf16[16,1024]{1,0:T(8,128)(2,1)}, u32[]{:S(2)}) copy-start(bf16[16,1024]{1,0:T(8,128)(2,1)} %constant.41.clone.ones_ref) | copy-start | bytes 98308
  0.0 7.5 %copy-start.1 = (bf16[1024,256]{1,0:T(8,128)(2,1)S(1)}, bf16[1024,256]{1,0:T(8,128)(2,1)}, u32[]{:S(2)}) copy-start(bf16[1024,256]{1,0:T(8,128)(2,1)} %constant.40.clone.wave_t_ref) | copy-start | bytes 1572868
  7.5 1.3 %copy-start = (bf16[1024,640]{1,0:T(8,128)(2,1)S(1)}, bf16[1024,640]{1,0:T(8,128)(2,1)}, u32[]{:S(2)}) copy-start(bf16[1024,640]{1,0:T(8,128)(2,1)} %reshape.107.x_ref) | copy-start | bytes 3932164
  8.8 1.0 %copy-start.2 = (bf16[256,1024]{1,0:T(8,128)(2,1)S(1)}, bf16[256,1024]{1,0:T(8,128)(2,1)}, u32[]{:S(2)}) copy-start(bf16[256,1024]{1,0:T(8,128)(2,1)} %constant.39.clone.wave_ref) | copy-start | bytes 1572868

commit v2 on v1

--- a/solution.py
+++ b/solution.py
@@ -13,6 +13,7 @@
 BAND_FREQS = 64
 MESH = pl.DeviceIdType.MESH
 LANES = 128
+DEPTH = 2
 F32 = jnp.float32
 BF16 = jnp.bfloat16
 
@@ -35,8 +36,8 @@
     return cast(wide), cast(wide.T), cast(ones)
 
 
-def kernel(sizes, x_ref, wave_ref, wave_t_ref, ones_ref, gain_ref, coef_ref, base_ref, out_ref,
-           held, part, other, ramp, acc, sums, est, near, cyc,
+def kernel(sizes, x_ref, wave_ref, wave_t_ref, ones_ref, shift_ref, band_ref, memory_ref, out_ref,
+           held, part, other, ramp, acc, sums, est, near, cyc, gain_ref, weight,
            z_send, c_send, recv, p_send, p_recv, s_send, s_recv, e_send, e_recv):
     T, C, R = sizes
     rows, width = x_ref.shape
@@ -104,9 +105,8 @@
 
     @pl.when(tm < T - 1)
     def _():
-        @pl.loop(0, chunks)
-        def _(j):
-            ahead(j).start()
+        for j in range(min(DEPTH, chunks)):
+            ahead(jnp.int32(j)).start()
 
     @pl.when(col == 0)
     def _():
@@ -125,7 +125,22 @@
 
     acc[...] = jnp.zeros_like(acc)
 
+    count = 2 * BAND_FREQS
+    index = lax.broadcasted_iota(jnp.int32, (R * count, 1), 0)
+    band = jnp.zeros((R * count, 1), F32)
+    for s in range(R):
+        band = jnp.where(index // count == s, band_ref[s].astype(F32), band)
+    freq = index % BAND_FREQS + 1
+    wave = freq.astype(F32)
+    gain = jnp.exp(-(wave * wave) / (2.0 * band * band)) * (2.0 / (2 * (rows // R)))
+    gain_ref[0] = gain
+    gain_ref[1] = jnp.where(freq % 2 == 1, -gain, gain)
+
     STEP = 32
+
+    target = lax.broadcasted_iota(jnp.int32, (1, total), 1) - shift_ref[0]
+    target = jnp.where(target < 0, target + total, target)
+    target = jnp.where(target >= total, target - total, target)
 
     @pl.loop(0, chunks)
     def _(j):
@@ -134,7 +149,7 @@
             def _(k):
                 m = lax.broadcasted_iota(jnp.int32, (STEP, total), 0) + (
                     c * width + j * LANES + k * STEP)
-                lag = base_ref[...] - m
+                lag = target - m
                 lag = jnp.where(lag < 0, lag + total, lag)
                 dist = jnp.minimum(lag, total - lag)
                 wide = jnp.maximum(dist, 1).astype(F32)
@@ -143,7 +158,12 @@
                     jnp.where((dist & 1) == 1, -1.0 / (math.pi**2 * wide * wide), 0.0))
                 ramp[j, pl.ds(pl.multiple_of(c * LANES + k * STEP, STEP), STEP), :] = tap.astype(BF16)
 
+    line_index = lax.broadcasted_iota(jnp.int32, (8, 1), 0)
+    decay = jnp.zeros((8, 1), F32)
+    for s in range(R):
+        decay = jnp.where(line_index == s, memory_ref[s], decay)
     est[...] = jnp.zeros_like(est)
+    weight[...] = jnp.zeros_like(weight)
     for u in range(T):
         @pl.when(u < tm)
         def _():
@@ -151,7 +171,10 @@
 
         @pl.when(u <= tm)
         def _():
-            est[...] += coef_ref[u] * sums[u]
+            both = sums[u] if u == 0 else sums[u - 1] + sums[u]
+            est[...] = decay * est[...] + both * (1.0 / (2 * (rows // R)))
+            weight[...] = decay * weight[...] + 1.0
+    est[...] = est[...] / weight[...]
     near[1, col] = est[...]
 
     def est_copy(delta, to_col, from_col):
@@ -182,10 +205,18 @@
         def _():
             bulk(j, jnp.int32(1), z_send, {"col": mate}).wait_recv()
 
+        @pl.when(tm < T - 1)
+        def _():
+            ahead(j).wait_send()
+
+            @pl.when(j + DEPTH < chunks)
+            def _():
+                ahead(j + DEPTH).start()
+
         part[j] = jnp.dot(wave_ref[...], held[j], preferred_element_type=F32)
         part_copy(j).start()
 
-    gather(0)
+    gather(jnp.int32(0))
 
     est_copy(0, mate, mate).wait_recv()
     for delta in (-1, 1):
@@ -252,10 +283,6 @@
     def _(j):
         part_copy(j).wait_send()
 
-        @pl.when(tm < T - 1)
-        def _():
-            ahead(j).wait_send()
-
         @pl.when(col == 0)
         def _():
             across(j).wait_send()
@@ -264,33 +291,17 @@
 def local(turns, shifts, bands, memory):
     half_len, R, width = turns.shape
     T, C = lax.axis_size("tm"), lax.axis_size("cuts")
-    tm = lax.axis_index("tm")
     rows, total, chunks = half_len * R, 2 * width, width // LANES
-    angle_count = 2 * half_len
     count = 2 * BAND_FREQS
     wide, wide_t, ones = tables(half_len, R)
     flat = turns.reshape(rows, width)
-
-    freq = np.arange(1, BAND_FREQS + 1, dtype=np.float32)
-    freq = np.concatenate([freq, freq])
-    sign = np.where(freq % 2 == 1, -1.0, 1.0).astype(np.float32)
-    gain = jnp.exp(-(freq[None, :] ** 2) / (2.0 * bands.astype(F32)[:, None] ** 2)) * (2.0 / angle_count)
-    gains = jnp.stack([gain.reshape(R * count, 1), (gain * sign[None, :]).reshape(R * count, 1)])
-
-    lag = tm - jnp.arange(T + 1, dtype=jnp.int32)
-    powers = jnp.where(
-        lag[:, None] >= 0,
-        jnp.power(memory[None, :], jnp.maximum(lag, 0).astype(F32)[:, None]), 0.0)
-    coef = (powers[:-1] + powers[1:]) / (jnp.sum(powers, axis=0)[None, :] * angle_count)
-    coef = jnp.pad(coef, ((0, 0), (0, 8 - R)))[:, :, None]
-    base = ((jnp.arange(total, dtype=jnp.int32) - shifts[0]) % total)[None, :]
 
     vmem = pl.BlockSpec(memory_space=pltpu.VMEM)
     dma = pltpu.SemaphoreType.DMA
     out = pl.pallas_call(
         functools.partial(kernel, (T, C, R)),
         out_shape=jax.ShapeDtypeStruct((rows, total), BF16),
-        in_specs=[vmem] * 7,
+        in_specs=[vmem] * 4 + [pl.BlockSpec(memory_space=pltpu.SMEM)] * 3,
         out_specs=vmem,
         scratch_shapes=[
             pltpu.VMEM((chunks, rows, 2 * LANES), BF16),
@@ -302,6 +313,8 @@
             pltpu.VMEM((8, width), F32),
             pltpu.VMEM((3, 2, 8, width), F32),
             pltpu.VMEM((chunks, 8, 2 * LANES), F32),
+            pltpu.VMEM((2, R * count, 1), F32),
+            pltpu.VMEM((8, 1), F32),
             dma((chunks,)), dma((chunks,)), dma((2, chunks)),
             dma((chunks,)), dma((chunks,)),
             dma((T,)), dma((T,)), dma((3, 2)), dma((3, 2)),
@@ -311,7 +324,7 @@
         cost_estimate=pl.CostEstimate(
             flops=2 * rows * total * (total + 2 * R * count),
             bytes_accessed=8 * rows * total, transcendentals=0),
-    )(flat, wide, wide_t, ones, gains, coef, base)
+    )(flat, wide, wide_t, ones, shifts, bands, memory)
     return out.reshape(half_len, R, total)
 
 

time: 51.9 us -> 50.3 us (0.969)
  the two profiles are of different devices: /device:TPU:12 before, /device:TPU:0 now
where the time goes in v2:
time: 50.3 us; the launch traced here: 50 us
  Pallas kernels  40.4 us (80%)
  local copies, waits for them, and re-layouts  8.88 us (18%)
  between operations  0.74 us (1%)
    pallas_call x1, Pallas kernels, local(): pl.pallas_call(functools.partial(kernel, (T, C, R)), out_shape=jax.ShapeD...  40.4 us
    reshape x1, local copies, waits for them, and re-layouts, local(): flat = turns.reshape(rows, width)  4.07 us
    reshape x1, local copies, waits for them, and re-layouts, local(): return out.reshape(half_len, R, total)  2.44 us
    unnamed x12, local copies, waits for them, and re-layouts  2.37 us

profile of v2, /device:TPU:0, one launch (start us, length us, event | category | flops | bytes accessed | tf_op | source)
XLA Modules:
  0.0 50.0 jit_solution(617190675910325825)
XLA Ops:
  0.0 0.0 copy-start.5
  0.0 0.0 copy-start.3
  0.0 0.0 copy-start.2
  0.0 0.0 copy-start.1
  0.7 4.1 %reshape.6.x_ref = bf16[1024,640]{1,0:T(8,128)(2,1)} reshape(bf16[512,2,640]{2,1,0:T(2,128)(2,1)} %param.7) | data formatting | bytes 2621440 | tf_op jit(solution)/shard_map/reshape | solution.py:297
  4.8 0.0 copy-done.5
  4.8 0.0 copy-done.3
  4.8 0.0 copy-done.2
  4.8 0.0 copy-done.1
  4.8 0.0 copy-start
  4.8 1.3 %copy-done = bf16[1024,640]{1,0:T(8,128)(2,1)S(1)} copy-done((bf16[1024,640]{1,0:T(8,128)(2,1)S(1)}, bf16[1024,640]{1,0:T(8,128)(2,1)}, u32[]{:S(2)}) %copy-start) | copy-done | bytes 1310744
  6.1 0.0 copy-start.4
  6.1 1.0 %copy-done.4 = bf16[256,1024]{1,0:T(8,128)(2,1)S(1)} copy-done((bf16[256,1024]{1,0:T(8,128)(2,1)S(1)}, bf16[256,1024]{1,0:T(8,128)(2,1)}, u32[]{:S(2)}) %copy-start.4) | copy-done | bytes 524312
  7.2 40.4 %shard_map.73 = bf16[1024,1280]{1,0:T(8,128)(2,1)S(1)} custom-call(bf16[1024,640]{1,0:T(8,128)(2,1)S(1)} %copy-done, bf16[256,1024]{1,0:T(8,128)(2,1)S(1)} %copy-done.4, bf16[1024,256]{1,0:T(8,128)(2,1)S(1)} %copy-done.3, bf16[16,1024]{1,0:T(8,128)(2,1)S(1)} %copy-done.5, s32[1]{0:T(128)S(6)} %copy.8.shift_ref, s32[2]{0:T(128)S(1)} %copy-done.1, f32[2]{0:T(128)S(1)} %copy-done.2), custom_call_target="tpu_custom_call" | custom-call | flops 4697620480 | bytes 10485760 | tf_op jit(solution)/shard_map/pallas_call | solution.py:301
  47.6 2.4 %reshape.7 = bf16[512,2,1280]{2,1,0:T(2,128)(2,1)} reshape(bf16[1024,1280]{1,0:T(8,128)(2,1)S(1)} %shard_map.73) | data formatting | bytes 5242880 | tf_op jit(solution)/shard_map/reshape | solution.py:328
Async XLA Ops:
  0.0 4.8 %copy-start.5 = (bf16[16,1024]{1,0:T(8,128)(2,1)S(1)}, bf16[16,1024]{1,0:T(8,128)(2,1)}, u32[]{:S(2)}) copy-start(bf16[16,1024]{1,0:T(8,128)(2,1)} %constant.8.clone.ones_ref) | copy-start | bytes 98308
  0.0 4.8 %copy-start.3 = (bf16[1024,256]{1,0:T(8,128)(2,1)S(1)}, bf16[1024,256]{1,0:T(8,128)(2,1)}, u32[]{:S(2)}) copy-start(bf16[1024,256]{1,0:T(8,128)(2,1)} %constant.7.clone.wave_t_ref) | copy-start | bytes 1572868
  0.0 4.8 %copy-start.2 = (f32[2]{0:T(128)S(1)}, f32[2]{0:T(128)}, u32[]{:S(2)}) copy-start(f32[2]{0:T(128)} %memory_ref.1) | copy-start | bytes 28
  0.0 4.8 %copy-start.1 = (s32[2]{0:T(128)S(1)}, s32[2]{0:T(128)}, u32[]{:S(2)}) copy-start(s32[2]{0:T(128)} %band_ref.1) | copy-start | bytes 28
  4.8 1.3 %copy-start = (bf16[1024,640]{1,0:T(8,128)(2,1)S(1)}, bf16[1024,640]{1,0:T(8,128)(2,1)}, u32[]{:S(2)}) copy-start(bf16[1024,640]{1,0:T(8,128)(2,1)} %reshape.6.x_ref) | copy-start | bytes 3932164
  6.1 1.0 %copy-start.4 = (bf16[256,1024]{1,0:T(8,128)(2,1)S(1)}, bf16[256,1024]{1,0:T(8,128)(2,1)}, u32[]{:S(2)}) copy-start(bf16[256,1024]{1,0:T(8,128)(2,1)} %constant.6.clone.wave_ref) | copy-start | bytes 1572868

commit v3 on v2

--- a/solution.py
+++ b/solution.py
@@ -37,18 +37,28 @@
 
 
 def kernel(sizes, x_ref, wave_ref, wave_t_ref, ones_ref, shift_ref, band_ref, memory_ref, out_ref,
-           held, part, other, ramp, acc, sums, est, near, cyc, gain_ref, weight,
-           z_send, c_send, recv, p_send, p_recv, s_send, s_recv, e_send, e_recv):
+           held, own, part, other, ramp, acc, sums, est, near, cyc, gain_ref, weight,
+           l_sem, z_send, c_send, recv, p_send, p_recv, s_send, s_recv, e_send, e_recv):
     T, C, R = sizes
-    rows, width = x_ref.shape
-    chunks = width // LANES
+    half_len, chunks, _, _ = x_ref.shape
+    rows, width = half_len * R, chunks * LANES
     total = 2 * width
     tm = lax.axis_index("tm")
     cut = lax.axis_index("cuts")
     col = lax.axis_index("col")
     mate = 1 - col
 
-    sums[tm] = jnp.dot(ones_ref[...], x_ref[...], preferred_element_type=F32)[:8]
+    def mine(j):
+        return pltpu.make_async_copy(x_ref.at[:, j], own.at[j], l_sem.at[0, j])
+
+    def kept(j):
+        return pltpu.make_async_copy(x_ref.at[:, j], held.at[j, 1], l_sem.at[1, j])
+
+    def flat(ref):
+        return ref.reshape(rows, LANES)
+
+    for j in range(chunks):
+        mine(j).start()
 
     barrier = pltpu.get_barrier_semaphore()
 
@@ -85,15 +95,10 @@
             send_sem=s_send.at[target], recv_sem=s_recv.at[source],
             device_id={"tm": target}, device_id_type=MESH)
 
-    for u in range(T):
-        @pl.when(u > tm)
-        def _():
-            sum_copy(tm, jnp.int32(u)).start()
-
     def bulk(j, source_col, send_sem, where):
         return pltpu.make_async_remote_copy(
-            src_ref=x_ref.at[:, pl.ds(pl.multiple_of(j * LANES, LANES), LANES)],
-            dst_ref=held.at[j, :, pl.ds(pl.multiple_of(source_col * LANES, LANES), LANES)],
+            src_ref=x_ref.at[:, j],
+            dst_ref=held.at[j, source_col],
             send_sem=send_sem.at[j], recv_sem=recv.at[source_col, j],
             device_id=where, device_id_type=MESH)
 
@@ -117,7 +122,17 @@
     @pl.when(col == 1)
     def _():
         for j in range(chunks):
-            held[j, :, LANES:] = x_ref[:, j * LANES:(j + 1) * LANES]
+            kept(j).start()
+
+    for j in range(chunks):
+        mine(j).wait()
+        sums[tm, :, j * LANES:(j + 1) * LANES] = jnp.dot(
+            ones_ref[...], flat(own.at[j])[...], preferred_element_type=F32)[:8]
+
+    for u in range(T):
+        @pl.when(u > tm)
+        def _():
+            sum_copy(tm, jnp.int32(u)).start()
 
     @pl.when((col == 0) & (tm == 0))
     def _():
@@ -213,7 +228,12 @@
             def _():
                 ahead(j + DEPTH).start()
 
-        part[j] = jnp.dot(wave_ref[...], held[j], preferred_element_type=F32)
+        @pl.when(col == 1)
+        def _():
+            kept(j).wait()
+
+        both = jnp.concatenate([flat(held.at[j, c])[...] for c in range(2)], axis=1)
+        part[j] = jnp.dot(wave_ref[...], both, preferred_element_type=F32)
         part_copy(j).start()
 
     gather(jnp.int32(0))
@@ -254,7 +274,8 @@
         def _(k):
             tile = pl.ds(pl.multiple_of(k * TILE, TILE), TILE)
             low = jnp.dot(wave_t_ref[tile, :], scaled, preferred_element_type=F32)
-            damped = (held[j, tile, :].astype(F32) - low - shade).astype(BF16)
+            both = jnp.concatenate([flat(held.at[j, c])[tile, :] for c in range(2)], axis=1)
+            damped = (both.astype(F32) - low - shade).astype(BF16)
             product = acc[tile, :] + jnp.dot(damped, ramp[j], preferred_element_type=F32)
             if last:
                 out_ref[tile, :] = product.astype(BF16)
@@ -294,17 +315,18 @@
     rows, total, chunks = half_len * R, 2 * width, width // LANES
     count = 2 * BAND_FREQS
     wide, wide_t, ones = tables(half_len, R)
-    flat = turns.reshape(rows, width)
+    pieces = turns.reshape(half_len, R, chunks, LANES).transpose(0, 2, 1, 3)
 
     vmem = pl.BlockSpec(memory_space=pltpu.VMEM)
     dma = pltpu.SemaphoreType.DMA
     out = pl.pallas_call(
         functools.partial(kernel, (T, C, R)),
         out_shape=jax.ShapeDtypeStruct((rows, total), BF16),
-        in_specs=[vmem] * 4 + [pl.BlockSpec(memory_space=pltpu.SMEM)] * 3,
+        in_specs=[pl.BlockSpec(memory_space=pl.ANY)] + [vmem] * 3 + [pl.BlockSpec(memory_space=pltpu.SMEM)] * 3,
         out_specs=vmem,
         scratch_shapes=[
-            pltpu.VMEM((chunks, rows, 2 * LANES), BF16),
+            pltpu.VMEM((chunks, 2, half_len, R, LANES), BF16),
+            pltpu.VMEM((chunks, half_len, R, LANES), BF16),
             pltpu.VMEM((chunks, R * count, 2 * LANES), F32),
             pltpu.VMEM((chunks, R * count, 2 * LANES), F32),
             pltpu.VMEM((chunks, 2 * LANES, total), BF16),
@@ -315,7 +337,7 @@
             pltpu.VMEM((chunks, 8, 2 * LANES), F32),
             pltpu.VMEM((2, R * count, 1), F32),
             pltpu.VMEM((8, 1), F32),
-            dma((chunks,)), dma((chunks,)), dma((2, chunks)),
+            dma((2, chunks)), dma((chunks,)), dma((chunks,)), dma((2, chunks)),
             dma((chunks,)), dma((chunks,)),
             dma((T,)), dma((T,)), dma((3, 2)), dma((3, 2)),
         ],
@@ -324,7 +346,7 @@
         cost_estimate=pl.CostEstimate(
             flops=2 * rows * total * (total + 2 * R * count),
             bytes_accessed=8 * rows * total, transcendentals=0),
-    )(flat, wide, wide_t, ones, shifts, bands, memory)
+    )(pieces, wide, wide_t, ones, shifts, bands, memory)
     return out.reshape(half_len, R, total)
 
 

time: 50.3 us -> 50.2 us (level)
  local copies, waits for them, and re-layouts: 8.88 us -> 7.9 us
  Pallas kernels: 40.4 us -> 41.3 us
    reshape x1 -> x0, local copies, waits for them, and re-layouts: 4.07 us -> none  [local(): flat = turns.reshape(rows, width)]
    unnamed x12, local copies, waits for them, and re-layouts: 2.37 us -> 5.46 us
    pallas_call x1, Pallas kernels: 40.4 us -> 41.3 us  [local(): pl.pallas_call(functools.partial(kernel, (T, C, R)), out_shape=jax.ShapeD...]
where the time goes in v3:
time: 50.2 us; the launch traced here: 49.8 us
  Pallas kernels  41.3 us (82%)
  local copies, waits for them, and re-layouts  7.9 us (16%)
  between operations  0.67 us (1%)
    pallas_call x1, Pallas kernels, local(): pl.pallas_call(functools.partial(kernel, (T, C, R)), out_shape=jax.ShapeD...  41.3 us
    unnamed x12, local copies, waits for them, and re-layouts  5.46 us
    reshape x1, local copies, waits for them, and re-layouts, local(): return out.reshape(half_len, R, total)  2.44 us

profile of v3, /device:TPU:0, one launch (start us, length us, event | category | flops | bytes accessed | tf_op | source)
XLA Modules:
  0.0 49.8 jit_solution(6318931309754989753)
XLA Ops:
  0.7 0.0 copy-start
  0.7 1.3 %copy-done = bf16[512,2,640]{2,1,0:T(2,128)(2,1)S(1)} copy-done((bf16[512,2,640]{2,1,0:T(2,128)(2,1)S(1)}, bf16[512,2,640]{2,1,0:T(2,128)(2,1)}, u32[]{:S(2)}) %copy-start) | copy-done | bytes 1310744
  2.0 0.0 copy-start.1
  2.0 0.7 %copy-done.1 = s32[2]{0:T(128)S(1)} copy-done((s32[2]{0:T(128)S(1)}, s32[2]{0:T(128)}, u32[]{:S(2)}) %copy-start.1) | copy-done | bytes 32
  2.6 0.0 copy-start.2
  2.6 0.7 %copy-done.2 = f32[2]{0:T(128)S(1)} copy-done((f32[2]{0:T(128)S(1)}, f32[2]{0:T(128)}, u32[]{:S(2)}) %copy-start.2) | copy-done | bytes 32
  3.3 0.0 copy-start.3
  3.3 1.0 %copy-done.3 = bf16[1024,256]{1,0:T(8,128)(2,1)S(1)} copy-done((bf16[1024,256]{1,0:T(8,128)(2,1)S(1)}, bf16[1024,256]{1,0:T(8,128)(2,1)}, u32[]{:S(2)}) %copy-start.3) | copy-done | bytes 524312
  4.3 0.0 copy-start.4
  4.3 1.0 %copy-done.4 = bf16[256,1024]{1,0:T(8,128)(2,1)S(1)} copy-done((bf16[256,1024]{1,0:T(8,128)(2,1)S(1)}, bf16[256,1024]{1,0:T(8,128)(2,1)}, u32[]{:S(2)}) %copy-start.4) | copy-done | bytes 524312
  5.4 0.0 copy-start.5
  5.4 0.8 %copy-done.5 = bf16[16,1024]{1,0:T(8,128)(2,1)S(1)} copy-done((bf16[16,1024]{1,0:T(8,128)(2,1)S(1)}, bf16[16,1024]{1,0:T(8,128)(2,1)}, u32[]{:S(2)}) %copy-start.5) | copy-done | bytes 32792
  6.1 41.3 %shard_map.73 = bf16[1024,1280]{1,0:T(8,128)(2,1)S(1)} custom-call(bf16[512,5,2,128]{3,2,1,0:T(2,128)(2,1)S(1)} %bitcast.3, bf16[256,1024]{1,0:T(8,128)(2,1)S(1)} %copy-done.4, bf16[1024,256]{1,0:T(8,128)(2,1)S(1)} %copy-done.3, bf16[16,1024]{1,0:T(8,128)(2,1)S(1)} %copy-done.5, s32[1]{0:T(128)S(6)} %copy.8.shift_ref, s32[2]{0:T(128)S(1)} %copy-done.1, ...), custom_call_target="tpu_custom_call" | custom-call | flops 4697620480 | bytes 10485760 | tf_op jit(solution)/shard_map/pallas_call | solution.py:322
  47.4 2.4 %reshape.7 = bf16[512,2,1280]{2,1,0:T(2,128)(2,1)} reshape(bf16[1024,1280]{1,0:T(8,128)(2,1)S(1)} %shard_map.73) | data formatting | bytes 5242880 | tf_op jit(solution)/shard_map/reshape | solution.py:350
Async XLA Ops:
  0.7 1.3 %copy-start = (bf16[512,2,640]{2,1,0:T(2,128)(2,1)S(1)}, bf16[512,2,640]{2,1,0:T(2,128)(2,1)}, u32[]{:S(2)}) copy-start(bf16[512,2,640]{2,1,0:T(2,128)(2,1)} %param.7) | copy-start | bytes 3932164
  2.0 0.7 %copy-start.1 = (s32[2]{0:T(128)S(1)}, s32[2]{0:T(128)}, u32[]{:S(2)}) copy-start(s32[2]{0:T(128)} %band_ref.1) | copy-start | bytes 28
  2.6 0.7 %copy-start.2 = (f32[2]{0:T(128)S(1)}, f32[2]{0:T(128)}, u32[]{:S(2)}) copy-start(f32[2]{0:T(128)} %memory_ref.1) | copy-start | bytes 28
  3.3 1.0 %copy-start.3 = (bf16[1024,256]{1,0:T(8,128)(2,1)S(1)}, bf16[1024,256]{1,0:T(8,128)(2,1)}, u32[]{:S(2)}) copy-start(bf16[1024,256]{1,0:T(8,128)(2,1)} %constant.7.clone.wave_t_ref) | copy-start | bytes 1572868
  4.3 1.0 %copy-start.4 = (bf16[256,1024]{1,0:T(8,128)(2,1)S(1)}, bf16[256,1024]{1,0:T(8,128)(2,1)}, u32[]{:S(2)}) copy-start(bf16[256,1024]{1,0:T(8,128)(2,1)} %constant.6.clone.wave_ref) | copy-start | bytes 1572868
  5.4 0.8 %copy-start.5 = (bf16[16,1024]{1,0:T(8,128)(2,1)S(1)}, bf16[16,1024]{1,0:T(8,128)(2,1)}, u32[]{:S(2)}) copy-start(bf16[16,1024]{1,0:T(8,128)(2,1)} %constant.8.clone.ones_ref) | copy-start | bytes 98308

commit v4 on v3

--- a/solution.py
+++ b/solution.py
@@ -13,7 +13,7 @@
 BAND_FREQS = 64
 MESH = pl.DeviceIdType.MESH
 LANES = 128
-DEPTH = 2
+DEPTH = 3
 F32 = jnp.float32
 BF16 = jnp.bfloat16
 
@@ -36,7 +36,8 @@
     return cast(wide), cast(wide.T), cast(ones)
 
 
-def kernel(sizes, x_ref, wave_ref, wave_t_ref, ones_ref, shift_ref, band_ref, memory_ref, out_ref,
+def kernel(sizes, x_ref, wave_hbm, wave_t_hbm, ones_hbm, shift_ref, band_ref, memory_ref, out_ref,
+           wave_ref, wave_t_ref, ones_ref, t_sem,
            held, own, part, other, ramp, acc, sums, est, near, cyc, gain_ref, weight,
            l_sem, z_send, c_send, recv, p_send, p_recv, s_send, s_recv, e_send, e_recv):
     T, C, R = sizes
@@ -59,6 +60,12 @@
 
     for j in range(chunks):
         mine(j).start()
+    load_ones = pltpu.make_async_copy(ones_hbm, ones_ref, t_sem.at[0])
+    load_wave = pltpu.make_async_copy(wave_hbm, wave_ref, t_sem.at[1])
+    load_wave_t = pltpu.make_async_copy(wave_t_hbm, wave_t_ref, t_sem.at[2])
+    load_ones.start()
+    load_wave.start()
+    load_wave_t.start()
 
     barrier = pltpu.get_barrier_semaphore()
 
@@ -124,6 +131,7 @@
         for j in range(chunks):
             kept(j).start()
 
+    load_ones.wait()
     for j in range(chunks):
         mine(j).wait()
         sums[tm, :, j * LANES:(j + 1) * LANES] = jnp.dot(
@@ -173,6 +181,41 @@
                     jnp.where((dist & 1) == 1, -1.0 / (math.pi**2 * wide * wide), 0.0))
                 ramp[j, pl.ds(pl.multiple_of(c * LANES + k * STEP, STEP), STEP), :] = tap.astype(BF16)
 
+    def part_copy(j):
+        return pltpu.make_async_remote_copy(
+            src_ref=part.at[j], dst_ref=other.at[j],
+            send_sem=p_send.at[j], recv_sem=p_recv.at[j],
+            device_id={"col": mate}, device_id_type=MESH)
+
+    def gather(j):
+        @pl.when((col == 1) | (tm > 0))
+        def _():
+            bulk(j, jnp.int32(0), z_send, {"col": mate}).wait_recv()
+
+        @pl.when((col == 0) & (tm > 0))
+        def _():
+            bulk(j, jnp.int32(1), z_send, {"col": mate}).wait_recv()
+
+        @pl.when(tm < T - 1)
+        def _():
+            ahead(j).wait_send()
+
+            @pl.when(j + DEPTH < chunks)
+            def _():
+                ahead(j + DEPTH).start()
+
+        @pl.when(col == 1)
+        def _():
+            kept(j).wait()
+
+        both = jnp.concatenate([flat(held.at[j, c])[...] for c in range(2)], axis=1)
+        part[j] = jnp.dot(wave_ref[...], both, preferred_element_type=F32)
+        part_copy(j).start()
+
+    load_wave.wait()
+    load_wave_t.wait()
+    gather(jnp.int32(0))
+
     line_index = lax.broadcasted_iota(jnp.int32, (8, 1), 0)
     decay = jnp.zeros((8, 1), F32)
     for s in range(R):
@@ -204,39 +247,6 @@
         def _():
             for c in range(2):
                 est_copy(delta, jnp.int32(c), col).start()
-
-    def part_copy(j):
-        return pltpu.make_async_remote_copy(
-            src_ref=part.at[j], dst_ref=other.at[j],
-            send_sem=p_send.at[j], recv_sem=p_recv.at[j],
-            device_id={"col": mate}, device_id_type=MESH)
-
-    def gather(j):
-        @pl.when((col == 1) | (tm > 0))
-        def _():
-            bulk(j, jnp.int32(0), z_send, {"col": mate}).wait_recv()
-
-        @pl.when((col == 0) & (tm > 0))
-        def _():
-            bulk(j, jnp.int32(1), z_send, {"col": mate}).wait_recv()
-
-        @pl.when(tm < T - 1)
-        def _():
-            ahead(j).wait_send()
-
-            @pl.when(j + DEPTH < chunks)
-            def _():
-                ahead(j + DEPTH).start()
-
-        @pl.when(col == 1)
-        def _():
-            kept(j).wait()
-
-        both = jnp.concatenate([flat(held.at[j, c])[...] for c in range(2)], axis=1)
-        part[j] = jnp.dot(wave_ref[...], both, preferred_element_type=F32)
-        part_copy(j).start()
-
-    gather(jnp.int32(0))
 
     est_copy(0, mate, mate).wait_recv()
     for delta in (-1, 1):
@@ -322,9 +332,10 @@
     out = pl.pallas_call(
         functools.partial(kernel, (T, C, R)),
         out_shape=jax.ShapeDtypeStruct((rows, total), BF16),
-        in_specs=[pl.BlockSpec(memory_space=pl.ANY)] + [vmem] * 3 + [pl.BlockSpec(memory_space=pltpu.SMEM)] * 3,
+        in_specs=[pl.BlockSpec(memory_space=pltpu.HBM)] * 4 + [pl.BlockSpec(memory_space=pltpu.SMEM)] * 3,
         out_specs=vmem,
         scratch_shapes=[
+            pltpu.VMEM(wide.shape, BF16), pltpu.VMEM(wide_t.shape, BF16), pltpu.VMEM(ones.shape, BF16), dma((3,)),
             pltpu.VMEM((chunks, 2, half_len, R, LANES), BF16),
             pltpu.VMEM((chunks, half_len, R, LANES), BF16),
             pltpu.VMEM((chunks, R * count, 2 * LANES), F32),
@@ -342,7 +353,7 @@
             dma((T,)), dma((T,)), dma((3, 2)), dma((3, 2)),
         ],
         compiler_params=pltpu.CompilerParams(
-            collective_id=0, has_side_effects=True, vmem_limit_bytes=48 * 1024 * 1024),
+            collective_id=0, has_side_effects=True, vmem_limit_bytes=60 * 1024 * 1024),
         cost_estimate=pl.CostEstimate(
             flops=2 * rows * total * (total + 2 * R * count),
             bytes_accessed=8 * rows * total, transcendentals=0),

time: 50.2 us -> 50.4 us (level); the launches traced: 49.8 us -> 49.5 us
  local copies, waits for them, and re-layouts: 7.9 us -> 6.45 us
  Pallas kernels: 41.3 us -> 42.4 us
    unnamed x12 -> x0, local copies, waits for them, and re-layouts: 5.46 us -> none
    reshape x1, local copies, waits for them, and re-layouts: 2.44 us -> 6.45 us  [local(): return out.reshape(half_len, R, total)]
    pallas_call x1, Pallas kernels: 41.3 us -> 42.4 us  [local(): pl.pallas_call(functools.partial(kernel, (T, C, R)), out_shape=jax.ShapeD...]
where the time goes in v4:
time: 50.4 us; the launch traced here: 49.5 us
  Pallas kernels  42.4 us (84%)
  local copies, waits for them, and re-layouts  6.45 us (13%)
  between operations  0.66 us (1%)
    pallas_call x1, Pallas kernels, local(): pl.pallas_call(functools.partial(kernel, (T, C, R)), out_shape=jax.ShapeD...  42.4 us
    reshape x1, local copies, waits for them, and re-layouts, local(): return out.reshape(half_len, R, total)  6.45 us

profile of v4, /device:TPU:0, one launch (start us, length us, event | category | flops | bytes accessed | tf_op | source)
XLA Modules:
  0.0 49.5 jit_solution(12258322559217716375)
XLA Ops:
  0.7 42.4 %shard_map.73 = bf16[1024,1280]{1,0:T(8,128)(2,1)} custom-call(bf16[512,5,2,128]{3,2,1,0:T(2,128)(2,1)} %bitcast.3, bf16[256,1024]{1,0:T(8,128)(2,1)} %constant.6.clone.wave_hbm, bf16[1024,256]{1,0:T(8,128)(2,1)} %constant.7.clone.wave_t_hbm, bf16[16,1024]{1,0:T(8,128)(2,1)} %constant.8.clone.ones_hbm, s32[1]{0:T(128)S(6)} %copy.8.shift_ref, s32[2]{0:T(128)} %band_ref.1, ...), custom_call_target="tpu_custom_call" | custom-call | flops 4697620480 | bytes 10485760 | tf_op jit(solution)/shard_map/pallas_call | solution.py:332
  43.0 6.4 %reshape.7 = bf16[512,2,1280]{2,1,0:T(2,128)(2,1)} reshape(bf16[1024,1280]{1,0:T(8,128)(2,1)} %shard_map.73) | data formatting | bytes 5242880 | tf_op jit(solution)/shard_map/reshape | solution.py:361
